TPU v7x, 32 devices: a whole 2x2x4 slice. The times are simulated.
32 devices in a mesh: dom: 2 (over x), fsdp: 8 (over z, y), dp: 2 (over core).
Axes of the slice: x: 2, y: 2, z: 4, core: 2. Of those that a mesh axis runs over, the one named last changes fastest.
Arguments:
- activations: bfloat16 [4096, 8192], P(('dom', 'fsdp', 'dp')), parts along dimension 0, may hold values from -6 to 6
- cotangents: bfloat16 [4096, 8192], P(('dom', 'fsdp', 'dp')), parts along dimension 0, may hold values from -6 to 6
- in_factor: bfloat16 [8192, 64], replicated, may hold values from -0.0625 to 0.0625
- out_factor: bfloat16 [8192, 128], replicated, may hold values from -0.0625 to 0.0625
- earlier: bfloat16 [1024, 8192], P(('dom', 'fsdp', 'dp')), parts along dimension 0, may hold values from -6 to 6
Outputs:
- features: bfloat16 [32, 8192], P(('dom', 'fsdp', 'dp')), parts along dimension 0
- gram: float32 [16384, 8192], P(('dom', 'fsdp', 'dp')), parts along dimension 0
There are 2 independent parts, one for each index of `dom`. A program takes and returns all parts, laid end to end along the dimension named above; an argument that names none is the same for every part. Nothing has to cross between parts.
All inputs are finite; a program needn't handle non-finite values.
Results may differ from a plain program's by a relative error of at most 0.0058.
Values may be sent and summed in bfloat16 or wider, within the bound.
A program may use at most 192 MiB of HBM per device.

v0:
```python
import jax
import jax.numpy as jnp
from jax import lax
from jax.sharding import PartitionSpec as P

LEN = 128


def on_device(activations, cotangents, in_factor, out_factor, earlier):
    rows = activations.shape[0]
    kin = in_factor.shape[1]
    kout = out_factor.shape[1]
    inner = jnp.dot(activations, in_factor, preferred_element_type=jnp.float32).astype(jnp.bfloat16)
    outer = jnp.dot(cotangents, out_factor, preferred_element_type=jnp.float32).astype(jnp.bfloat16)
    seq_count = rows // LEN
    blocks = jnp.einsum(
        "sta,stb->sab",
        outer.reshape(seq_count, LEN, kout),
        inner.reshape(seq_count, LEN, kin),
        preferred_element_type=jnp.float32,
    )
    features = (blocks.reshape(seq_count, kout * kin) * LEN ** (-0.5)).astype(jnp.bfloat16)
    width = earlier.shape[1]
    total_rows = earlier.shape[0] * lax.axis_size("fsdp") * lax.axis_size("dp")
    dims = (((0,), (0,)), ((), ()))
    owned = width // lax.axis_size("fsdp")
    offset = lax.axis_index("fsdp") * owned
    piece = lax.all_gather(earlier, "fsdp", axis=0, tiled=True)
    cols = lax.dynamic_slice_in_dim(piece, offset, owned, 1)
    partial_rows = lax.dot_general(cols, piece, dims, preferred_element_type=jnp.float32)
    summed = lax.psum_scatter(partial_rows, "dp", scatter_dimension=0, tiled=True)
    gram = summed / total_rows
    return (features, gram)


def solution(mesh):
    placed = (
        P(("dom", "fsdp", "dp"), None),
        P(("dom", "fsdp", "dp"), None),
        P(),
        P(),
        P(("dom", "fsdp", "dp"), None),
    )
    return jax.shard_map(
        on_device,
        mesh=mesh,
        in_specs=placed,
        out_specs=(P(("dom", "fsdp", "dp"), None), P(("dom", "fsdp", "dp"), None)),
        check_vma=False,
    )
```

profile of v0, /device:TPU:0, one launch (start us, length us, event | category | flops | bytes accessed | tf_op | source)
XLA Modules:
  0.0 166.5 jit_solution(5068564062369680844)
XLA Ops:
  7.2 0.0 copy-start
  7.2 0.0 all-gather.2.cloned.1.call-start
  7.2 0.7 all-gather.2.cloned.1.call-update
  7.9 0.0 reduce-scatter.2.cloned.1.call-start
  8.0 78.3 %all-gather.2.cloned.1.call-done = bf16[256,8192]{1,0:T(8,128)(2,1)} async-done(((bf16[32,8192]{1,0:T(8,128)(2,1)}), bf16[256,8192]{1,0:T(8,128)(2,1)}) %all-gather.2.cloned.1.call-update) | async-done | bytes 4194320 | tf_op jit(solution)/shard_map/all_gather | solution.py:28
  86.3 18.0 %fusion.3 = f32[1024,8192]{1,0:T(8,128)} fusion(bf16[256,8192]{1,0:T(8,128)(2,1)} %all-gather.2.cloned.1.call-done, s32[]{:T(128)S(6)} %select_n.3), kind=kOutput, calls=%fused_computation.6 | convolution fusion | flops 4294967296 | bytes 38273028 | tf_op jit(solution)/shard_map/dot_general | solution.py:30
  104.3 0.0 copy-start.1
  104.3 0.0 reduce-scatter.2.cloned.1.call-update
  104.3 0.0 copy-done
  104.3 1.2 copy-done.1
  105.5 0.7 convolution_convert_fusion
  106.2 3.0 %fusion.2 = bf16[128,64]{0,1:T(8,128)(2,1)S(1)} fusion(bf16[128,64]{1,0:T(8,128)(2,1)S(1)} %convolution_convert_fusion, bf16[128,8192]{1,0:T(8,128)(2,1)} %param.6, bf16[8192,128]{1,0:T(8,128)(2,1)} %param.8), kind=kOutput, calls=%fused_computation.5 | convolution fusion | flops 270565376 | bytes 4227072 | tf_op jit(solution)/shard_map/sta,stb->sab/dot_general | solution.py:16
  109.2 0.1 copy.7
  109.3 0.7 convert_element_type.23
  110.1 37.9 %reduce-scatter.2.cloned.1.call-done = f32[512,8192]{1,0:T(8,128)} async-done(((f32[1024,8192]{1,0:T(8,128)}), f32[512,8192]{1,0:T(8,128)}) %reduce-scatter.2.cloned.1.call-update) | async-done | bytes 16777232 | tf_op jit(solution)/shard_map/reduce_scatter | solution.py:31
  148.0 11.6 %broadcast_multiply_fusion = f32[512,8192]{1,0:T(8,128)} fusion(f32[512,8192]{1,0:T(8,128)} %reduce-scatter.2.cloned.1.call-done), kind=kLoop, calls=%fused_computation | loop fusion | flops 4194304 | bytes 33554432 | tf_op jit(solution)/shard_map/div | solution.py:32
Async XLA Ops:
  7.2 97.1 %copy-start = (bf16[128,8192]{1,0:T(8,128)(2,1)S(1)}, bf16[128,8192]{1,0:T(8,128)(2,1)}, u32[]{:S(2)}) copy-start(bf16[128,8192]{1,0:T(8,128)(2,1)} %param.5) | copy-start | bytes 6291460
  7.2 79.1 %all-gather.2.cloned.1.call-start = ((), (), s32[]{:S(2)}) async-start(), calls=%async_computation.1 | async-start | bytes 4718592 | tf_op jit(solution)/shard_map/all_gather | solution.py:28
  7.9 140.1 %reduce-scatter.2.cloned.1.call-start = ((), (), s32[]{:S(2)}) async-start(), calls=%async_computation.2 | async-start | bytes 50331648 | tf_op jit(solution)/shard_map/reduce_scatter | solution.py:31
  104.3 1.2 copy-start.1
Sparse Core Ops, SparseCore 0:
  10.1 76.0 all-gather.1
  104.4 43.5 reduce-scatter.1
where the time goes:
time: 167 us; the launch traced here: 166 us
  waiting for transfers between devices  117 us (70%)
  matrix products  21.7 us (13%)
  between operations  14.1 us (8%)
  other arithmetic  11.6 us (7%)
  local copies, waits for them, and re-layouts  2.04 us (1%)
    all_gather x1, waiting for transfers between devices, on_device(): piece = lax.all_gather(earlier, 'fsdp', axis=0, tiled=True)  78.3 us
    reduce_scatter x1, waiting for transfers between devices, on_device(): lax.psum_scatter(partial_rows, 'dp', scatter_dimension=0, tiled=True)  37.9 us
    dot_general x1, matrix products, on_device(): lax.dot_general(cols, piece, dims, preferred_element_type=jnp.float32)  18 us
    div x1, other arithmetic, on_device(): gram = summed / total_rows  11.6 us
  transfers between devices with their start and end apart: 2, of which 2 were waited for; matrix products, arithmetic and copies ran while one was open for 3% of the time, Pallas kernels for 0%

commit v1 on v0

v1 whole, which is shorter than its diff:
```python
import functools

import jax
import jax.numpy as jnp
from jax import lax
from jax.experimental import pallas as pl
from jax.experimental.pallas import tpu as pltpu
from jax.sharding import PartitionSpec as P

LEN = 128
AXES = ("fsdp", "dp")
MIB = 1 << 20
CHUNKS = 4
DEPTH = 4
SIDES = 2


def gather_kernel(act_ref, cot_ref, inf_ref, outf_ref, own_ref, all_ref, feat_ref,
                  act, cot, inf, outf, flat, blk, up_sem, down_sem, side_sem, core_sem,
                  ici_sem, pair_sem, own_sem, load_sem):
    dom, f, c = lax.axis_index("dom"), lax.axis_index("fsdp"), lax.axis_index("dp")
    z, y = f // SIDES, f % SIDES
    rows, width = own_ref.shape
    step = width // CHUNKS
    last = DEPTH - 1
    far = range(CHUNKS // 2)
    near = range(CHUNKS // 2, CHUNKS)

    def device(zz, yy, cc):
        return (dom, zz * SIDES + yy, cc)

    up, down = device(jnp.minimum(z + 1, last), y, c), device(jnp.maximum(z - 1, 0), y, c)
    side, pair = device(z, 1 - y, c), device(z, y, 1 - c)
    has_up, has_down = z < last, z > 0

    loads = [pltpu.make_async_copy(s, d, load_sem.at[i])
             for i, (s, d) in enumerate(((act_ref, act), (cot_ref, cot), (inf_ref, inf), (outf_ref, outf)))]
    for copy in loads:
        copy.start()

    barrier = pltpu.get_barrier_semaphore()

    def greet(to):
        pl.semaphore_signal(barrier, inc=1, device_id=to, device_id_type=pl.DeviceIdType.MESH)

    pl.when(has_up)(lambda: greet(up))
    pl.when(has_down)(lambda: greet(down))
    greet(side)
    greet(pair)
    pl.semaphore_wait(barrier, 2 + has_up.astype(jnp.int32) + has_down.astype(jnp.int32))

    def place(ff, cc, k):
        start = pl.multiple_of((ff * 2 + cc) * rows, rows)
        return all_ref.at[pl.ds(start, rows), pl.ds(k * step, step)]

    def send(sems, ff, k, to, own=False):
        src = own_ref.at[:, pl.ds(k * step, step)] if own else place(ff, c, k)
        recv = pair_sem if sems is core_sem else ici_sem
        return pltpu.make_async_remote_copy(
            src_ref=src, dst_ref=place(ff, c, k), send_sem=sems.at[ff, k], recv_sem=recv.at[ff, k],
            device_id=to, device_id_type=pl.DeviceIdType.MESH)

    sent = []

    def go(sems, ff, k, to, cond=None, own=False):
        copy = send(sems, ff, k, to, own)
        if cond is None:
            copy.start()
        else:
            pl.when(cond)(lambda: copy.start())
        sent.append((cond, copy))

    def arrive(ff, k, cond):
        pl.when(cond)(lambda: send(side_sem, ff, k, side).wait_recv())

    keep = pltpu.make_async_copy(own_ref, all_ref.at[pl.ds(pl.multiple_of((f * 2 + c) * rows, rows), rows)], own_sem)
    for k in range(CHUNKS):
        go(up_sem, f, k, up, has_up, True)
        go(down_sem, f, k, down, has_down, True)
        go(side_sem, f, k, side, None, True)
    for k in range(CHUNKS):
        go(core_sem, f, k, pair, None, True)
    keep.start()

    for copy in loads:
        copy.wait()
    kin, kout = inf.shape[1], outf.shape[1]
    part = width // 8

    def project(i, totals):
        at = pl.ds(pl.multiple_of(i * part, part), part)
        return (totals[0] + jnp.dot(act[:, at], inf[at, :], preferred_element_type=jnp.float32),
                totals[1] + jnp.dot(cot[:, at], outf[at, :], preferred_element_type=jnp.float32))

    inner, outer = lax.fori_loop(0, 8, project, (jnp.zeros((LEN, kin), jnp.float32), jnp.zeros((LEN, kout), jnp.float32)))
    inner, outer = inner.astype(jnp.bfloat16), outer.astype(jnp.bfloat16)
    blk[...] = lax.dot_general(outer, inner, (((0,), (0,)), ((), ())), preferred_element_type=jnp.float32) * LEN ** (-0.5)
    wide = jnp.concatenate([blk[pl.ds(0, kout // 2, 2), :], blk[pl.ds(1, kout // 2, 2), :]], axis=1)
    for a in range(kout // 2):
        flat[0:1, 2 * kin * a:2 * kin * (a + 1)] = wide[a:a + 1, :]
    feat_ref[...] = flat[...].astype(feat_ref.dtype)

    def beside(ff):
        return ff + 1 - 2 * y

    for s in range(1, DEPTH + 1):
        below, above = z - s, z + s
        f_below, f_above = jnp.maximum(below, 0) * SIDES + y, jnp.minimum(above, last) * SIDES + y
        if s <= last:
            has_b, has_a = below >= 0, above <= last
            for k in range(CHUNKS):
                arrive(f_below, k, has_b)
                go(up_sem, f_below, k, up, has_b & has_up)
                across = has_b & (below != 0) if k in far else has_b
                go(side_sem, f_below, k, side, across)
                go(core_sem, f_below, k, pair, has_b)
                arrive(f_above, k, has_a)
                go(down_sem, f_above, k, down, has_a & has_down)
                across = has_a & (above != last) if k in far else has_a
                go(side_sem, f_above, k, side, across)
                go(core_sem, f_above, k, pair, has_a)
        for ff, here, to, on, sems in ((0 * SIDES + 1 - y, z == s - 1, up, has_up, up_sem),
                                       (last * SIDES + 1 - y, z == last - (s - 1), down, has_down, down_sem)):
            for k in far:
                arrive(ff, k, here)
                go(sems, ff, k, to, here & on)
                go(core_sem, ff, k, pair, here)
        d = s - 1
        for k in (*near, *far):
            for zz in ((z,) if d == 0 else (z - d, z + d)):
                ok = (zz >= 0) & (zz <= last)
                if k in far:
                    ok = ok & (zz != 0) & (zz != last)
                ff = jnp.clip(zz, 0, last) * SIDES + 1 - y
                arrive(ff, k, ok)
                go(core_sem, ff, k, pair, ok)

    for cond, copy in sent:
        if cond is None:
            copy.wait_send()
        else:
            pl.when(cond)(lambda copy=copy: copy.wait_send())
    keep.wait()
    for ff in range(DEPTH * SIDES):
        for k in range(CHUNKS):
            pltpu.make_async_remote_copy(
                src_ref=place(ff, 1 - c, k), dst_ref=place(ff, 1 - c, k), send_sem=core_sem.at[ff, k],
                recv_sem=pair_sem.at[ff, k], device_id=pair, device_id_type=pl.DeviceIdType.MESH).wait_recv()


def gather(activations, cotangents, in_factor, out_factor, earlier):
    rows, width = earlier.shape
    devices = DEPTH * SIDES * 2
    kin, kout = in_factor.shape[1], out_factor.shape[1]
    hbm = pl.BlockSpec(memory_space=pl.ANY)
    dma = pltpu.SemaphoreType.DMA
    chips = DEPTH * SIDES
    return pl.pallas_call(
        gather_kernel,
        name="gather_and_features",
        out_shape=(jax.ShapeDtypeStruct((rows * devices, width), earlier.dtype),
                   jax.ShapeDtypeStruct((1, kin * kout), jnp.bfloat16)),
        in_specs=[hbm] * 5,
        out_specs=(hbm, pl.BlockSpec(memory_space=pltpu.VMEM)),
        scratch_shapes=[
            pltpu.VMEM(activations.shape, activations.dtype),
            pltpu.VMEM(cotangents.shape, cotangents.dtype),
            pltpu.VMEM(in_factor.shape, in_factor.dtype),
            pltpu.VMEM(out_factor.shape, out_factor.dtype),
            pltpu.VMEM((1, kin * kout), jnp.float32),
            pltpu.VMEM((kout, kin), jnp.float32),
            *[dma((chips, CHUNKS))] * 6,
            dma(()),
            dma((4,)),
        ],
        compiler_params=pltpu.CompilerParams(collective_id=1, has_side_effects=True, vmem_limit_bytes=24 * MIB),
    )(activations, cotangents, in_factor, out_factor, earlier)


def gram_kernel(scale, cols_ref, tile_ref, feat_ref, gram_ref, out_feat_ref, turned):
    @pl.when(pl.program_id(0) == 0)
    def _():
        turned[...] = cols_ref[...].T
        out_feat_ref[...] = feat_ref[...]

    gram_ref[...] = jnp.dot(turned[...], tile_ref[...], preferred_element_type=jnp.float32) * scale


def gram_of(everything, features):
    total, width = everything.shape
    assert total & (total - 1) == 0
    owned = width // (lax.axis_size("fsdp") * lax.axis_size("dp"))
    tile = 1024
    whole = pl.BlockSpec(features.shape, lambda j: (0, 0))
    return pl.pallas_call(
        functools.partial(gram_kernel, 1.0 / total),
        name="gram",
        grid=(width // tile,),
        out_shape=(jax.ShapeDtypeStruct((owned, width), jnp.float32),
                   jax.ShapeDtypeStruct(features.shape, features.dtype)),
        in_specs=[pl.BlockSpec((total, owned), lambda j: (0, lax.axis_index("fsdp") * 2 + lax.axis_index("dp"))),
                  pl.BlockSpec((total, tile), lambda j: (0, j)), whole],
        out_specs=(pl.BlockSpec((owned, tile), lambda j: (0, j)), whole),
        scratch_shapes=[pltpu.VMEM((owned, total), everything.dtype)],
        compiler_params=pltpu.CompilerParams(vmem_limit_bytes=24 * MIB),
    )(everything, everything, features)


def plain_features(activations, cotangents, in_factor, out_factor):
    inner = jnp.dot(activations, in_factor, preferred_element_type=jnp.float32).astype(jnp.bfloat16)
    outer = jnp.dot(cotangents, out_factor, preferred_element_type=jnp.float32).astype(jnp.bfloat16)
    kin, kout = inner.shape[1], outer.shape[1]
    blocks = jnp.einsum("sta,stb->sab", outer.reshape(-1, LEN, kout), inner.reshape(-1, LEN, kin),
                        preferred_element_type=jnp.float32)
    return (blocks.reshape(-1, kout * kin) * LEN ** (-0.5)).astype(jnp.bfloat16)


def on_device(activations, cotangents, in_factor, out_factor, earlier):
    if lax.axis_size("fsdp") == DEPTH * SIDES and activations.shape[0] == LEN:
        everything, features = gather(activations, cotangents, in_factor, out_factor, earlier)
    else:
        everything = lax.all_gather(earlier, AXES, axis=0, tiled=True)
        features = plain_features(activations, cotangents, in_factor, out_factor)
    gram, features = gram_of(everything, features)
    return features, gram


def solution(mesh):
    rows = P(("dom", "fsdp", "dp"), None)
    return jax.shard_map(
        on_device,
        mesh=mesh,
        in_specs=(rows, rows, P(), P(), rows),
        out_specs=(rows, rows),
        check_vma=False,
    )
```

time: 167 us -> 65.3 us (0.39)
  waiting for transfers between devices: 117 us -> 0 us
  Pallas kernels: 0 us -> 57.6 us
  matrix products: 21.7 us -> 0 us
  between operations: 14.1 us -> 0.67 us
  other arithmetic: 11.6 us -> 0 us
  local copies, waits for them, and re-layouts: 2.04 us -> 6.86 us
    all_gather x1 -> x0, waiting for transfers between devices: 78.3 us -> none  [on_device(): piece = lax.all_gather(earlier, 'fsdp', axis=0, tiled=True)]
    pallas_call x0 -> x2, Pallas kernels: none -> 57.6 us  [the longest x1 48.1 us: gather(): pl.pallas_call(gather_kernel, name='gather_and_features', out_shape=(jax....]
    reduce_scatter x1 -> x0, waiting for transfers between devices: 37.9 us -> none  [on_device(): lax.psum_scatter(partial_rows, 'dp', scatter_dimension=0, tiled=True)]
    dot_general x3 -> x0, matrix products: 21.7 us -> none  [the longest x1 18 us: on_device(): lax.dot_general(cols, piece, dims, preferred_element_type=jnp.float32)]
    div x1 -> x0, other arithmetic: 11.6 us -> none  [on_device(): gram = summed / total_rows]
    unnamed x4 -> x9, local copies, waits for them, and re-layouts: 1.2 us -> 6.86 us
  transfers between devices with their start and end apart: 2 -> 0, of which waited for: 2 -> 0; matrix products, arithmetic and copies ran while one was open for 3% -> 0% of each run, Pallas kernels for 0% -> 0%
where the time goes in v1:
time: 65.3 us; the launch traced here: 65.1 us
  Pallas kernels  57.6 us (88%)
  local copies, waits for them, and re-layouts  6.86 us (11%)
  between operations  0.67 us (1%)
    pallas_call x1, Pallas kernels, gather(): pl.pallas_call(gather_kernel, name='gather_and_features', out_shape=(jax....  48.1 us
    pallas_call x1, Pallas kernels, gram_of(): pl.pallas_call(functools.partial(gram_kernel, 1.0 / total), name='gram',...  9.5 us
    unnamed x9, local copies, waits for them, and re-layouts  6.86 us

profile of v1, /device:TPU:0, one launch (start us, length us, event | category | flops | bytes accessed | tf_op | source)
XLA Modules:
  0.0 65.1 jit_solution(18218765652970745874)
XLA Ops:
  0.6 0.0 copy-start.3
  0.6 2.1 %copy.7.inf_ref = bf16[8192,64]{1,0:T(8,128)(2,1)S(1)} copy(bf16[8192,64]{0,1:T(8,128)(2,1)} %param.7) | data formatting | bytes 2097152 | tf_op args[2]
  2.7 0.0 copy-done.3
  2.7 0.0 copy-start
  2.8 1.6 %copy-done = bf16[128,8192]{1,0:T(8,128)(2,1)S(1)} copy-done((bf16[128,8192]{1,0:T(8,128)(2,1)S(1)}, bf16[128,8192]{1,0:T(8,128)(2,1)}, u32[]{:S(2)}) %copy-start) | copy-done | bytes 2097176
  4.3 0.0 copy-start.1
  4.3 1.6 %copy-done.1 = bf16[128,8192]{1,0:T(8,128)(2,1)S(1)} copy-done((bf16[128,8192]{1,0:T(8,128)(2,1)S(1)}, bf16[128,8192]{1,0:T(8,128)(2,1)}, u32[]{:S(2)}) %copy-start.1) | copy-done | bytes 2097176
  5.9 0.0 copy-start.2
  5.9 1.6 %copy-done.2 = bf16[8192,128]{1,0:T(8,128)(2,1)S(1)} copy-done((bf16[8192,128]{1,0:T(8,128)(2,1)S(1)}, bf16[8192,128]{1,0:T(8,128)(2,1)}, u32[]{:S(2)}) %copy-start.2) | copy-done | bytes 2097176
  7.5 48.1 %gather_and_features.1 = (bf16[512,8192]{1,0:T(8,128)(2,1)S(1)}, bf16[1,8192]{1,0:T(2,128)(2,1)S(1)}) custom-call(bf16[128,8192]{1,0:T(8,128)(2,1)S(1)} %copy-done, bf16[128,8192]{1,0:T(8,128)(2,1)S(1)} %copy-done.1, bf16[8192,64]{1,0:T(8,128)(2,1)S(1)} %copy.7.inf_ref, bf16[8192,128]{1,0:T(8,128)(2,1)S(1)} %copy-done.2, bf16[32,8192]{1,0:T(8,128)(2,1)S(1)} %copy-done.3), custom_call_target="tpu_custom_call" | custom-call | tf_op jit(solution)/shard_map/gather_and_features/pallas_call | solution.py:158
  55.6 9.5 %gram.1 = (f32[512,8192]{1,0:T(8,128)}, bf16[1,8192]{1,0:T(2,128)(2,1)}) custom-call(bf16[512,8192]{1,0:T(8,128)(2,1)S(1)} %get-tuple-element.6.cols_ref.tile_ref, bf16[512,8192]{1,0:T(8,128)(2,1)S(1)} %get-tuple-element.6.cols_ref.tile_ref, bf16[1,8192]{1,0:T(2,128)(2,1)S(1)} %get-tuple-element.7.feat_ref), custom_call_target="tpu_custom_call" | custom-call | tf_op jit(solution)/shard_map/gram/pallas_call | solution.py:195
Async XLA Ops:
  0.6 2.1 %copy-start.3 = (bf16[32,8192]{1,0:T(8,128)(2,1)S(1)}, bf16[32,8192]{1,0:T(8,128)(2,1)}, u32[]{:S(2)}) copy-start(bf16[32,8192]{1,0:T(8,128)(2,1)} %own_ref.1) | copy-start | bytes 1572868
  2.7 1.6 %copy-start = (bf16[128,8192]{1,0:T(8,128)(2,1)S(1)}, bf16[128,8192]{1,0:T(8,128)(2,1)}, u32[]{:S(2)}) copy-start(bf16[128,8192]{1,0:T(8,128)(2,1)} %act_ref.1) | copy-start | bytes 6291460
  4.3 1.6 %copy-start.1 = (bf16[128,8192]{1,0:T(8,128)(2,1)S(1)}, bf16[128,8192]{1,0:T(8,128)(2,1)}, u32[]{:S(2)}) copy-start(bf16[128,8192]{1,0:T(8,128)(2,1)} %cot_ref.1) | copy-start | bytes 6291460
  5.9 1.6 %copy-start.2 = (bf16[8192,128]{1,0:T(8,128)(2,1)S(1)}, bf16[8192,128]{1,0:T(8,128)(2,1)}, u32[]{:S(2)}) copy-start(bf16[8192,128]{1,0:T(8,128)(2,1)} %outf_ref.1) | copy-start | bytes 6291460

commit v2 on v1

v2 whole, which is shorter than its diff:
```python
import functools

import jax
import jax.numpy as jnp
from jax import lax
from jax.experimental import pallas as pl
from jax.experimental.pallas import tpu as pltpu
from jax.sharding import PartitionSpec as P

LEN = 128
AXES = ("fsdp", "dp")
MIB = 1 << 20
CHUNKS = 4
AHEAD = 8
LAG = 0.5
PIECES = 16
GATHER_VMEM = 52 * MIB
GRAM_VMEM = 28 * MIB
DEPTH = 4
SIDES = 2


def plan():
    last, half = DEPTH - 1, range(CHUNKS // 2)
    whole = range(CHUNKS)
    queue = {}
    for z in range(DEPTH):
        if z < last:
            queue[z, "up"] = [(0, s, k) for s in range(z, -1, -1) for k in whole] + [(1, 0, k) for k in half]
        if z > 0:
            queue[z, "down"] = [(0, s, k) for s in range(z, DEPTH) for k in whole] + [(1, last, k) for k in half]
        queue[z, "side"] = [(0, s, k) for d in range(DEPTH) for k in whole for s in sorted({z - d, z + d})
                            if 0 <= s <= last and (s == z or s not in (0, last) or k not in half)]
    here = {(z, (0, z, k)): 0.0 for z in range(DEPTH) for k in whole}
    free = dict.fromkeys(queue, 0.0)
    left = {q: list(items) for q, items in queue.items()}
    order = {q: [] for q in queue}
    while any(left.values()):
        at, q, p = min((max(free[q], here[q[0], p]), q, n) for q, items in left.items()
                       for n, p in enumerate(items) if (q[0], p) in here)
        p = left[q].pop(p)
        free[q] = at + 1
        order[q].append((at + 1, p))
        z, link = q
        to, line = {"up": (z + 1, p[0]), "down": (z - 1, p[0]), "side": (z, 1 - p[0])}[link]
        here[to, (line, *p[1:])] = at + 1 + LAG

    programs = []
    for z in range(DEPTH):
        events = [(0.0, 1, ("start", "core", (0, z, k))) for k in whole] + [(0.0, 2, ("features", None, None))]
        for (to, p), at in here.items():
            if to == z and p[:2] != (0, z):
                events += [(at, 3, ("arrived", "side", p)), (at, 5, ("start", "core", p))]
        for link in ("up", "down", "side"):
            done = order.get((z, link), [])
            for n, (end, p) in enumerate(done):
                before = done[n - AHEAD] if n >= AHEAD else (0.0, None)
                at = max(here[z, p], before[0])
                if before[1] is not None:
                    events.append((at, 4, ("sent", link, before[1])))
                events.append((at, 0 if at == 0 else 4, ("start", link, p)))
        steps = [step for _, _, step in sorted(events, key=lambda e: e[:2])]
        waited = {s[1:] for s in steps if s[0] == "sent"}
        steps += [("sent", *s[1:]) for s in steps if s[0] == "start" and s[1:] not in waited]
        programs.append(steps)
    return programs


def gather_kernel(act_ref, cot_ref, inf_ref, outf_ref, own_ref, all_ref, feat_ref,
                  act, cot, inf, outf, flat, blk, up_sem, down_sem, side_sem, core_sem,
                  ici_sem, pair_sem, own_sem, load_sem):
    dom, f, c = lax.axis_index("dom"), lax.axis_index("fsdp"), lax.axis_index("dp")
    z, y = f // SIDES, f % SIDES
    rows, width = own_ref.shape
    step = width // CHUNKS
    last = DEPTH - 1

    def device(zz, yy, cc):
        return (dom, zz * SIDES + yy, cc)

    up, down = device(jnp.minimum(z + 1, last), y, c), device(jnp.maximum(z - 1, 0), y, c)
    side, pair = device(z, 1 - y, c), device(z, y, 1 - c)
    has_up, has_down = z < last, z > 0

    loads = [pltpu.make_async_copy(s, d, load_sem.at[i])
             for i, (s, d) in enumerate(((act_ref, act), (cot_ref, cot), (inf_ref, inf), (outf_ref, outf)))]
    for copy in loads:
        copy.start()

    barrier = pltpu.get_barrier_semaphore()

    def greet(to):
        pl.semaphore_signal(barrier, inc=1, device_id=to, device_id_type=pl.DeviceIdType.MESH)

    pl.when(has_up)(lambda: greet(up))
    pl.when(has_down)(lambda: greet(down))
    greet(side)
    greet(pair)
    pl.semaphore_wait(barrier, 2 + has_up.astype(jnp.int32) + has_down.astype(jnp.int32))

    def place(ff, cc, k):
        start = pl.multiple_of((ff * 2 + cc) * rows, rows)
        return all_ref.at[pl.ds(start, rows), pl.ds(k * step, step)]

    keep = pltpu.make_async_copy(own_ref, all_ref.at[pl.ds(pl.multiple_of((f * 2 + c) * rows, rows), rows)], own_sem)
    keep.start()

    def features():
        for copy in loads:
            copy.wait()
        kin, kout = inf.shape[0], outf.shape[1]
        part = width // 8

        def project(i, totals):
            at = pl.ds(pl.multiple_of(i * part, part), part)
            return (totals[0] + lax.dot_general(act[:, at], inf[:, at], (((1,), (1,)), ((), ())), preferred_element_type=jnp.float32),
                    totals[1] + jnp.dot(cot[:, at], outf[at, :], preferred_element_type=jnp.float32))

        inner, outer = lax.fori_loop(0, 8, project, (jnp.zeros((LEN, kin), jnp.float32), jnp.zeros((LEN, kout), jnp.float32)))
        inner, outer = inner.astype(jnp.bfloat16), outer.astype(jnp.bfloat16)
        blk[...] = lax.dot_general(outer, inner, (((0,), (0,)), ((), ())), preferred_element_type=jnp.float32) * LEN ** (-0.5)
        wide = jnp.concatenate([blk[pl.ds(0, kout // 2, 2), :], blk[pl.ds(1, kout // 2, 2), :]], axis=1)
        for a in range(kout // 2):
            flat[0:1, 2 * kin * a:2 * kin * (a + 1)] = wide[a:a + 1, :]
        feat_ref[...] = flat[...].astype(feat_ref.dtype)

    links = {"up": (up_sem, up), "down": (down_sem, down), "side": (side_sem, side), "core": (core_sem, pair)}

    def run(row, program):
        def remote(link, piece):
            line, source, k = piece
            ff = source * SIDES + (y if line == 0 else 1 - y)
            sems, to = links[link]
            src = own_ref.at[:, pl.ds(k * step, step)] if (line, source) == (0, row) else place(ff, c, k)
            return pltpu.make_async_remote_copy(
                src_ref=src, dst_ref=place(ff, c, k), send_sem=sems.at[ff, k],
                recv_sem=(pair_sem if link == "core" else ici_sem).at[ff, k],
                device_id=to, device_id_type=pl.DeviceIdType.MESH)

        for what, link, piece in program:
            if what == "features":
                features()
            elif what == "start":
                remote(link, piece).start()
            elif what == "sent":
                remote(link, piece).wait_send()
            else:
                remote(link, piece).wait_recv()

    for row, program in enumerate(plan()):
        pl.when(z == row)(functools.partial(run, row, program))

    keep.wait()
    for ff in range(DEPTH * SIDES):
        for k in range(CHUNKS):
            pltpu.make_async_remote_copy(
                src_ref=place(ff, 1 - c, k), dst_ref=place(ff, 1 - c, k), send_sem=core_sem.at[ff, k],
                recv_sem=pair_sem.at[ff, k], device_id=pair, device_id_type=pl.DeviceIdType.MESH).wait_recv()


def gather(activations, cotangents, in_factor, out_factor, earlier):
    rows, width = earlier.shape
    devices = DEPTH * SIDES * 2
    kin, kout = in_factor.shape[1], out_factor.shape[1]
    hbm = pl.BlockSpec(memory_space=pltpu.HBM)
    dma = pltpu.SemaphoreType.DMA
    chips = DEPTH * SIDES
    return pl.pallas_call(
        gather_kernel,
        name="gather_and_features",
        out_shape=(pltpu.VMEM((rows * devices, width), earlier.dtype),
                   pltpu.VMEM((1, kin * kout), jnp.bfloat16)),
        in_specs=[hbm] * 5,
        out_specs=(pl.BlockSpec(memory_space=pl.ANY), pl.BlockSpec(memory_space=pltpu.VMEM)),
        scratch_shapes=[
            pltpu.VMEM(activations.shape, activations.dtype),
            pltpu.VMEM(cotangents.shape, cotangents.dtype),
            pltpu.VMEM(in_factor.shape[::-1], in_factor.dtype),
            pltpu.VMEM(out_factor.shape, out_factor.dtype),
            pltpu.VMEM((1, kin * kout), jnp.float32),
            pltpu.VMEM((kout, kin), jnp.float32),
            *[dma((chips, CHUNKS))] * 6,
            dma(()),
            dma((4,)),
        ],
        compiler_params=pltpu.CompilerParams(collective_id=1, has_side_effects=True, vmem_limit_bytes=GATHER_VMEM),
    )(activations, cotangents, in_factor.T, out_factor, earlier)


def gram_kernel(scale, all_ref, feat_ref, gram_ref, out_feat_ref, turned, tiles, sems):
    owned, width = gram_ref.shape
    pieces = PIECES
    tile = width // pieces
    me = lax.axis_index("fsdp") * lax.axis_size("dp") + lax.axis_index("dp")
    out_feat_ref[...] = feat_ref[...]
    turned[...] = all_ref[:, pl.ds(pl.multiple_of(me * owned, owned), owned)].T
    copies = []
    for j in range(pieces):
        at = pl.ds(j * tile, tile)
        tiles[:, at] = jnp.dot(turned[...], all_ref[:, at], preferred_element_type=jnp.float32) * scale
        copies.append(pltpu.make_async_copy(tiles.at[:, at], gram_ref.at[:, at], sems.at[j]))
        copies[-1].start()
    for copy in copies:
        copy.wait()


def gram_of(everything, features):
    total, width = everything.shape
    assert total & (total - 1) == 0
    owned = width // (lax.axis_size("fsdp") * lax.axis_size("dp"))
    vmem = pl.BlockSpec(memory_space=pltpu.VMEM)
    return pl.pallas_call(
        functools.partial(gram_kernel, 1.0 / total),
        name="gram",
        out_shape=(jax.ShapeDtypeStruct((owned, width), jnp.float32),
                   jax.ShapeDtypeStruct(features.shape, features.dtype)),
        in_specs=[vmem, vmem],
        out_specs=(pl.BlockSpec(memory_space=pl.ANY), vmem),
        scratch_shapes=[pltpu.VMEM((owned, total), everything.dtype),
                        pltpu.VMEM((owned, width), jnp.float32),
                        pltpu.SemaphoreType.DMA((PIECES,))],
        compiler_params=pltpu.CompilerParams(vmem_limit_bytes=GRAM_VMEM),
    )(everything, features)


def plain_features(activations, cotangents, in_factor, out_factor):
    inner = jnp.dot(activations, in_factor, preferred_element_type=jnp.float32).astype(jnp.bfloat16)
    outer = jnp.dot(cotangents, out_factor, preferred_element_type=jnp.float32).astype(jnp.bfloat16)
    kin, kout = inner.shape[1], outer.shape[1]
    blocks = jnp.einsum("sta,stb->sab", outer.reshape(-1, LEN, kout), inner.reshape(-1, LEN, kin),
                        preferred_element_type=jnp.float32)
    return (blocks.reshape(-1, kout * kin) * LEN ** (-0.5)).astype(jnp.bfloat16)


def plain_gram(earlier):
    everything = lax.all_gather(earlier, AXES, axis=0, tiled=True)
    total, width = everything.shape
    devices = lax.axis_size("fsdp") * lax.axis_size("dp")
    owned = width // devices
    me = lax.axis_index("fsdp") * lax.axis_size("dp") + lax.axis_index("dp")
    cols = lax.dynamic_slice_in_dim(everything, me * owned, owned, 1)
    return lax.dot_general(cols, everything, (((0,), (0,)), ((), ())), preferred_element_type=jnp.float32) / total


def on_device(activations, cotangents, in_factor, out_factor, earlier):
    if lax.axis_size("fsdp") == DEPTH * SIDES and activations.shape[0] == LEN:
        everything, features = gather(activations, cotangents, in_factor, out_factor, earlier)
        gram, features = gram_of(everything, features)
        return features, gram
    return plain_features(activations, cotangents, in_factor, out_factor), plain_gram(earlier)


def solution(mesh):
    rows = P(("dom", "fsdp", "dp"), None)
    return jax.shard_map(
        on_device,
        mesh=mesh,
        in_specs=(rows, rows, P(), P(), rows),
        out_specs=(rows, rows),
        check_vma=False,
    )
```

time: 65.3 us -> 55.5 us (0.85)
  local copies, waits for them, and re-layouts: 6.86 us -> 0 us
  Pallas kernels: 57.6 us -> 54.7 us
    unnamed x9 -> x0, local copies, waits for them, and re-layouts: 6.86 us -> none
    pallas_call x1, Pallas kernels: 9.5 us -> 7.06 us  [gram_of(): pl.pallas_call(functools.partial(gram_kernel, 1.0 / total), name='gram',...]
where the time goes in v2:
time: 55.5 us; the launch traced here: 55.3 us
  Pallas kernels  54.7 us (99%)
  between operations  0.64 us (1%)
    pallas_call x1, Pallas kernels, gather(): pl.pallas_call(gather_kernel, name='gather_and_features', out_shape=(pltp...  47.6 us
    pallas_call x1, Pallas kernels, gram_of(): pl.pallas_call(functools.partial(gram_kernel, 1.0 / total), name='gram',...  7.06 us

profile of v2, /device:TPU:0, one launch (start us, length us, event | category | flops | bytes accessed | tf_op | source)
XLA Modules:
  0.0 55.3 jit_solution(15384006136363566183)
XLA Ops:
  0.6 47.6 %gather_and_features.1 = (bf16[512,8192]{1,0:T(8,128)(2,1)S(1)}, bf16[1,8192]{1,0:T(2,128)(2,1)S(1)}) custom-call(bf16[128,8192]{1,0:T(8,128)(2,1)} %act_ref.1, bf16[128,8192]{1,0:T(8,128)(2,1)} %cot_ref.1, bf16[64,8192]{1,0:T(8,128)(2,1)} %bitcast.1, bf16[8192,128]{1,0:T(8,128)(2,1)} %outf_ref.1, bf16[32,8192]{1,0:T(8,128)(2,1)} %own_ref.1), custom_call_target="tpu_custom_call" | custom-call | tf_op jit(solution)/shard_map/gather_and_features/pallas_call | solution.py:168
  48.3 7.1 %gram.1 = (f32[512,8192]{1,0:T(8,128)}, bf16[1,8192]{1,0:T(2,128)(2,1)}) custom-call(bf16[512,8192]{1,0:T(8,128)(2,1)S(1)} %get-tuple-element.6.all_ref, bf16[1,8192]{1,0:T(2,128)(2,1)S(1)} %get-tuple-element.7.feat_ref), custom_call_target="tpu_custom_call" | custom-call | tf_op jit(solution)/shard_map/gram/pallas_call | solution.py:212

commit v3 on v2

--- a/solution.py
+++ b/solution.py
@@ -84,9 +84,6 @@
 
     loads = [pltpu.make_async_copy(s, d, load_sem.at[i])
              for i, (s, d) in enumerate(((act_ref, act), (cot_ref, cot), (inf_ref, inf), (outf_ref, outf)))]
-    for copy in loads:
-        copy.start()
-
     barrier = pltpu.get_barrier_semaphore()
 
     def greet(to):
@@ -96,6 +93,8 @@
     pl.when(has_down)(lambda: greet(down))
     greet(side)
     greet(pair)
+    for copy in loads:
+        copy.start()
     pl.semaphore_wait(barrier, 2 + has_up.astype(jnp.int32) + has_down.astype(jnp.int32))
 
     def place(ff, cc, k):
@@ -103,7 +102,6 @@
         return all_ref.at[pl.ds(start, rows), pl.ds(k * step, step)]
 
     keep = pltpu.make_async_copy(own_ref, all_ref.at[pl.ds(pl.multiple_of((f * 2 + c) * rows, rows), rows)], own_sem)
-    keep.start()
 
     def features():
         for copy in loads:
@@ -139,6 +137,7 @@
 
         for what, link, piece in program:
             if what == "features":
+                keep.start()
                 features()
             elif what == "start":
                 remote(link, piece).start()

time: 55.5 us -> 55.5 us (level)
  no operation moved by 1% of the time
where the time goes in v3:
time: 55.5 us; the launch traced here: 55.3 us
  Pallas kernels  54.7 us (99%)
  between operations  0.64 us (1%)
    pallas_call x1, Pallas kernels, gather(): pl.pallas_call(gather_kernel, name='gather_and_features', out_shape=(pltp...  47.6 us
    pallas_call x1, Pallas kernels, gram_of(): pl.pallas_call(functools.partial(gram_kernel, 1.0 / total), name='gram',...  7.06 us

profile of v3, /device:TPU:0, one launch (start us, length us, event | category | flops | bytes accessed | tf_op | source)
XLA Modules:
  0.0 55.3 jit_solution(10368448418786417301)
XLA Ops:
  0.6 47.6 %gather_and_features.1 = (bf16[512,8192]{1,0:T(8,128)(2,1)S(1)}, bf16[1,8192]{1,0:T(2,128)(2,1)S(1)}) custom-call(bf16[128,8192]{1,0:T(8,128)(2,1)} %act_ref.1, bf16[128,8192]{1,0:T(8,128)(2,1)} %cot_ref.1, bf16[64,8192]{1,0:T(8,128)(2,1)} %bitcast.1, bf16[8192,128]{1,0:T(8,128)(2,1)} %outf_ref.1, bf16[32,8192]{1,0:T(8,128)(2,1)} %own_ref.1), custom_call_target="tpu_custom_call" | custom-call | tf_op jit(solution)/shard_map/gather_and_features/pallas_call | solution.py:167
  48.2 7.1 %gram.1 = (f32[512,8192]{1,0:T(8,128)}, bf16[1,8192]{1,0:T(2,128)(2,1)}) custom-call(bf16[512,8192]{1,0:T(8,128)(2,1)S(1)} %get-tuple-element.6.all_ref, bf16[1,8192]{1,0:T(2,128)(2,1)S(1)} %get-tuple-element.7.feat_ref), custom_call_target="tpu_custom_call" | custom-call | tf_op jit(solution)/shard_map/gram/pallas_call | solution.py:211
